TPU v7x, 32 devices: a whole 2x2x4 slice. The times are simulated.
32 devices in a mesh: clip: 8 (over y, x, core), tok: 4 (over z).
Axes of the slice: x: 2, y: 2, z: 4, core: 2. Of those that a mesh axis runs over, the one named last changes fastest.
Arguments:
- frames: bfloat16 [8, 8, 196, 768], P('clip', 'tok'), may hold values from -6 to 6
- cotangent: bfloat16 [8, 8, 196, 768], P('clip', 'tok'), may hold values from -6 to 6
- entry_weights: float32 [27648, 128], P(('clip', 'tok')), may hold values from -0.21875 to 0.21875
- entry_momentum: float32 [27648, 128], P(('clip', 'tok')), may hold values from -640 to 640
- entry_variance: float32 [27648, 128], P(('clip', 'tok')), may hold values from 12544 to 50176
- temporal_weights: float32 [9216, 128], P(('clip', 'tok')), may hold values from -0.3125 to 0.3125
- temporal_momentum: float32 [9216, 128], P(('clip', 'tok')), may hold values from -640 to 640
- temporal_variance: float32 [9216, 128], P(('clip', 'tok')), may hold values from 12544 to 50176
- spatial_weights: float32 [4608, 128], P(('clip', 'tok')), may hold values from -1.75 to 1.75
- spatial_momentum: float32 [4608, 128], P(('clip', 'tok')), may hold values from -96 to 96
- spatial_variance: float32 [4608, 128], P(('clip', 'tok')), may hold values from 250.88 to 1003.52
- widen_weights: float32 [18432, 128], P(('clip', 'tok')), may hold values from -0.21875 to 0.21875
- widen_momentum: float32 [18432, 128], P(('clip', 'tok')), may hold values from -192 to 192
- widen_variance: float32 [18432, 128], P(('clip', 'tok')), may hold values from 1254.4 to 5017.6
- narrow_weights: float32 [18432, 128], P(('clip', 'tok')), may hold values from -0.109375 to 0.109375
- narrow_momentum: float32 [18432, 128], P(('clip', 'tok')), may hold values from -448 to 448
- narrow_variance: float32 [18432, 128], P(('clip', 'tok')), may hold values from 5017.6 to 20070.4
- norm_affine: float32 [2, 3, 768], P(None, None, ('clip', 'tok')), may hold values from -0.5 to 1.3, as said below
- affine_momentum: float32 [2, 3, 768], P(None, None, ('clip', 'tok')), may hold values from -640 to 640
- affine_variance: float32 [2, 3, 768], P(None, None, ('clip', 'tok')), may hold values from 12544 to 50176
Outputs:
- layer_output: bfloat16 [8, 8, 196, 768], P('clip', 'tok')
- input_gradient: float32 [8, 8, 196, 768], P('clip', 'tok')
- entry_updated: float32 [27648, 128], P(('clip', 'tok'))
- entry_averaged: float32 [27648, 128], P(('clip', 'tok'))
- entry_squared: float32 [27648, 128], P(('clip', 'tok'))
- temporal_updated: float32 [9216, 128], P(('clip', 'tok'))
- temporal_averaged: float32 [9216, 128], P(('clip', 'tok'))
- temporal_squared: float32 [9216, 128], P(('clip', 'tok'))
- spatial_updated: float32 [4608, 128], P(('clip', 'tok'))
- spatial_averaged: float32 [4608, 128], P(('clip', 'tok'))
- spatial_squared: float32 [4608, 128], P(('clip', 'tok'))
- widen_updated: float32 [18432, 128], P(('clip', 'tok'))
- widen_averaged: float32 [18432, 128], P(('clip', 'tok'))
- widen_squared: float32 [18432, 128], P(('clip', 'tok'))
- narrow_updated: float32 [18432, 128], P(('clip', 'tok'))
- narrow_averaged: float32 [18432, 128], P(('clip', 'tok'))
- narrow_squared: float32 [18432, 128], P(('clip', 'tok'))
- affine_updated: float32 [2, 3, 768], P(None, None, ('clip', 'tok'))
- affine_averaged: float32 [2, 3, 768], P(None, None, ('clip', 'tok'))
- affine_squared: float32 [2, 2, 768], P(None, None, ('clip', 'tok'))
- feed_squared: float32 [2, 768], P(None, ('clip', 'tok'))
Inputs may be any that keep to these rules, and one draw needn't show every extreme that they name: `norm_affine`: index 0 of the first dimension holds gains, index 1 biases.
All inputs are finite; a program needn't handle non-finite values.
Results may differ from a plain program's by a relative error of at most 0.02.
The roundings to bfloat16 on the way count: a program that leaves them out, or rounds other values in their place, can miss the bound.
Values may be sent and summed in bfloat16 or wider, within the bound.
A program may use at most 192 MiB of HBM per device.

v0:
```python
import jax
import jax.numpy as jnp
from jax import lax
from jax.sharding import PartitionSpec as P

D = 768
HEADS = 12
HEAD_DIM = 64
HID = 3072
PATCHES = 196
STEP = 5


time_scores = "cfphe,cgphe->cphfg"
time_mixed = "cphfg,cgphe->cfphe"
time_flip = "cphfg,cfphe->cgphe"
space_scores = "cfphe,cfqhe->cfhpq"
space_mixed = "cfhpq,cfqhe->cfphe"
space_flip = "cfhpq,cfphe->cfqhe"


def project(inputs, weight):
    return jnp.einsum("cfpa,ab->cfpb", inputs, weight, preferred_element_type=jnp.float32)


def project_back(upstream, weight):
    return jnp.einsum("cfpb,ab->cfpa", upstream, weight, preferred_element_type=jnp.float32)


def weight_sum(inputs, upstream):
    return jnp.einsum("cfpa,cfpb->ab", inputs, upstream, preferred_element_type=jnp.float32)


def layer_norm(values, gain, shift):
    center = values - jnp.mean(values, axis=-1, keepdims=True)
    inverse = lax.rsqrt(jnp.mean(center * center, axis=-1, keepdims=True) + 1e-06)
    unit = center * inverse
    return (unit * gain + shift, unit, inverse)


def norm_back(upstream, unit, inverse, gain):
    scaled = upstream * gain
    inner = (
        scaled
        - jnp.mean(scaled, axis=-1, keepdims=True)
        - unit * jnp.mean(scaled * unit, axis=-1, keepdims=True)
    )
    return (
        inner * inverse,
        jnp.sum(upstream * unit, axis=(0, 1, 2)),
        jnp.sum(upstream, axis=(0, 1, 2)),
    )


def split_heads(merged):
    lowered = merged.astype(jnp.bfloat16)
    parts = lowered.reshape(lowered.shape[:-1] + (3, HEADS, HEAD_DIM))
    return (parts[..., 0, :, :], parts[..., 1, :, :], parts[..., 2, :, :])


def attend_forward(heads, score_form, mixed_form):
    query, keys, values = heads
    scores = jnp.einsum(score_form, query, keys, preferred_element_type=jnp.float32) * HEAD_DIM ** (
        -0.5
    )
    top = jnp.max(scores, axis=-1, keepdims=True)
    expo = jnp.exp(scores - top)
    total = jnp.sum(expo, axis=-1, keepdims=True)
    probs = (expo / total).astype(jnp.bfloat16)
    mixed = jnp.einsum(mixed_form, probs, values, preferred_element_type=jnp.float32)
    joined = mixed.reshape(mixed.shape[:-2] + (HEADS * HEAD_DIM,)).astype(jnp.bfloat16)
    return (joined, top + jnp.log(total))


def attend_backward(heads, logsum, upstream_joined, score_form, mixed_form, flip_form):
    query, keys, values = heads
    upstream = upstream_joined.reshape(upstream_joined.shape[:-1] + (HEADS, HEAD_DIM))
    scale = HEAD_DIM ** (-0.5)
    scores = jnp.einsum(score_form, query, keys, preferred_element_type=jnp.float32) * scale
    probs = jnp.exp(scores - logsum)
    dprobs = jnp.einsum(score_form, upstream, values, preferred_element_type=jnp.float32)
    dscores = (probs * (dprobs - jnp.sum(dprobs * probs, axis=-1, keepdims=True))).astype(
        jnp.bfloat16
    )
    dquery = jnp.einsum(mixed_form, dscores, keys, preferred_element_type=jnp.float32) * scale
    dkeys = jnp.einsum(flip_form, dscores, query, preferred_element_type=jnp.float32) * scale
    dvalues = jnp.einsum(
        flip_form, probs.astype(jnp.bfloat16), upstream, preferred_element_type=jnp.float32
    )
    stacked = jnp.stack([dquery, dkeys, dvalues], axis=-3)
    return stacked.reshape(stacked.shape[:-3] + (3 * HEADS * HEAD_DIM,)).astype(jnp.bfloat16)


def collect(masters):
    gathered = (
        lax.all_gather(masters[0].astype(jnp.bfloat16), ("clip", "tok"), axis=0, tiled=True),
        lax.all_gather(masters[1].astype(jnp.bfloat16), ("clip", "tok"), axis=0, tiled=True),
        lax.all_gather(masters[2].astype(jnp.bfloat16), ("clip", "tok"), axis=0, tiled=True),
        lax.all_gather(masters[3].astype(jnp.bfloat16), ("clip", "tok"), axis=0, tiled=True),
        lax.all_gather(masters[4].astype(jnp.bfloat16), ("clip", "tok"), axis=0, tiled=True),
        lax.all_gather(masters[5].astype(jnp.bfloat16), ("clip", "tok"), axis=2, tiled=True),
    )
    return (
        gathered[0].reshape(2, D, 3 * D),
        gathered[1].reshape(2, D, D),
        gathered[2].reshape(D, D),
        gathered[3].reshape(D, HID),
        gathered[4].reshape(HID, D),
        gathered[5],
    )


def forward(frames, masters):
    weights = collect(masters)
    entry, temporal, spatial, widen, narrow, affine = weights
    gains = affine.astype(jnp.float32)
    patchwise = lax.all_to_all(frames, "tok", split_axis=2, concat_axis=1, tiled=True)
    normed_t, unit_t, inverse_t = layer_norm(
        patchwise.astype(jnp.float32), gains[0, 0], gains[1, 0]
    )
    lowered_t = normed_t.astype(jnp.bfloat16)
    heads_t = split_heads(project(lowered_t, entry[0]))
    mixed_t, lse_t = attend_forward(heads_t, time_scores, time_mixed)
    first_t = project(mixed_t, temporal[0]).astype(jnp.bfloat16)
    branch = project(first_t, temporal[1]).astype(jnp.bfloat16)
    returned = lax.all_to_all(branch, "tok", split_axis=1, concat_axis=2, tiled=True)
    after_t = frames.astype(jnp.float32) + returned.astype(jnp.float32)
    normed_s, unit_s, inverse_s = layer_norm(after_t, gains[0, 1], gains[1, 1])
    lowered_s = normed_s.astype(jnp.bfloat16)
    heads_s = split_heads(project(lowered_s, entry[1]))
    mixed_s, lse_s = attend_forward(heads_s, space_scores, space_mixed)
    after_s = after_t + project(mixed_s, spatial)
    normed_m, unit_m, inverse_m = layer_norm(after_s, gains[0, 2], gains[1, 2])
    lowered_m = normed_m.astype(jnp.bfloat16)
    widened = project(lowered_m, widen)
    activated = jax.nn.gelu(widened, approximate=False).astype(jnp.bfloat16)
    result = (after_s + project(activated, narrow)).astype(jnp.bfloat16)
    saved = {
        "weights": weights,
        "unit_t": unit_t,
        "inverse_t": inverse_t,
        "lowered_t": lowered_t,
        "heads_t": heads_t,
        "lse_t": lse_t,
        "mixed_t": mixed_t,
        "first_t": first_t,
        "unit_s": unit_s,
        "inverse_s": inverse_s,
        "lowered_s": lowered_s,
        "heads_s": heads_s,
        "lse_s": lse_s,
        "mixed_s": mixed_s,
        "unit_m": unit_m,
        "inverse_m": inverse_m,
        "lowered_m": lowered_m,
        "widened": widened,
        "activated": activated,
    }
    return (result, saved)


def adamw(master, moment, square, grad, rate):
    fix = 1.0 - 0.5**STEP
    averaged = 0.5 * moment + 0.5 * grad
    squared = 0.5 * square + 0.5 * grad * grad
    updated = master - rate * (averaged / fix / (jnp.sqrt(squared / fix) + 1e-08) + 0.1 * master)
    return (updated, averaged, squared)


def on_device(
    frames,
    cotangent,
    entry_weights,
    entry_momentum,
    entry_variance,
    temporal_weights,
    temporal_momentum,
    temporal_variance,
    spatial_weights,
    spatial_momentum,
    spatial_variance,
    widen_weights,
    widen_momentum,
    widen_variance,
    narrow_weights,
    narrow_momentum,
    narrow_variance,
    norm_affine,
    affine_momentum,
    affine_variance,
):
    masters = (
        entry_weights,
        temporal_weights,
        spatial_weights,
        widen_weights,
        narrow_weights,
        norm_affine,
    )
    result, unused = forward(frames, masters)
    fenced = lax.optimization_barrier((frames, masters, result))
    again, saved = forward(fenced[0], fenced[1])
    entry, temporal, spatial, widen, narrow, affine = saved["weights"]
    gains = affine.astype(jnp.float32)
    narrow_grad = weight_sum(saved["activated"], cotangent)
    widened = saved["widened"]
    slope = (
        0.5 * (1.0 + lax.erf(widened * 0.7071067811865476))
        + widened * jnp.exp(-0.5 * widened * widened) * 0.3989422804014327
    )
    dwidened = (project_back(cotangent, narrow) * slope).astype(jnp.bfloat16)
    widen_grad = weight_sum(saved["lowered_m"], dwidened)
    dpart_m, gain_m, shift_m = norm_back(
        project_back(dwidened, widen), saved["unit_m"], saved["inverse_m"], gains[0, 2]
    )
    dafter_s = cotangent.astype(jnp.float32) + dpart_m
    dspatial = dafter_s.astype(jnp.bfloat16)
    spatial_grad = weight_sum(saved["mixed_s"], dspatial)
    dmixed_s = project_back(dspatial, spatial).astype(jnp.bfloat16)
    dfused_s = attend_backward(
        saved["heads_s"], saved["lse_s"], dmixed_s, space_scores, space_mixed, space_flip
    )
    entry_grad_s = weight_sum(saved["lowered_s"], dfused_s)
    dpart_s, gain_s, shift_s = norm_back(
        project_back(dfused_s, entry[1]), saved["unit_s"], saved["inverse_s"], gains[0, 1]
    )
    dafter_t = dafter_s + dpart_s
    dbranch = lax.all_to_all(
        dafter_t.astype(jnp.bfloat16), "tok", split_axis=2, concat_axis=1, tiled=True
    )
    temporal_grad_b = weight_sum(saved["first_t"], dbranch)
    dfirst = project_back(dbranch, temporal[1]).astype(jnp.bfloat16)
    temporal_grad_a = weight_sum(saved["mixed_t"], dfirst)
    dmixed_t = project_back(dfirst, temporal[0]).astype(jnp.bfloat16)
    dfused_t = attend_backward(
        saved["heads_t"], saved["lse_t"], dmixed_t, time_scores, time_mixed, time_flip
    )
    entry_grad_t = weight_sum(saved["lowered_t"], dfused_t)
    dsent, gain_t, shift_t = norm_back(
        project_back(dfused_t, entry[0]), saved["unit_t"], saved["inverse_t"], gains[0, 0]
    )
    dreturned = lax.all_to_all(
        dsent.astype(jnp.bfloat16), "tok", split_axis=1, concat_axis=2, tiled=True
    )
    input_gradient = dafter_t + dreturned.astype(jnp.float32)
    members = (
        jnp.stack([entry_grad_t, entry_grad_s]).reshape(-1, 128),
        jnp.stack([temporal_grad_a, temporal_grad_b]).reshape(-1, 128),
        spatial_grad.reshape(-1, 128),
        widen_grad.reshape(-1, 128),
        narrow_grad.reshape(-1, 128),
        jnp.stack([jnp.stack([gain_t, gain_s, gain_m]), jnp.stack([shift_t, shift_s, shift_m])]),
    )
    totals = (
        lax.psum_scatter(members[0], ("clip", "tok"), scatter_dimension=0, tiled=True),
        lax.psum_scatter(members[1], ("clip", "tok"), scatter_dimension=0, tiled=True),
        lax.psum_scatter(members[2], ("clip", "tok"), scatter_dimension=0, tiled=True),
        lax.psum_scatter(members[3], ("clip", "tok"), scatter_dimension=0, tiled=True),
        lax.psum_scatter(members[4], ("clip", "tok"), scatter_dimension=0, tiled=True),
        lax.psum_scatter(members[5], ("clip", "tok"), scatter_dimension=2, tiled=True),
    )
    entry_sum, temporal_sum, spatial_sum, widen_sum, narrow_sum, affine_sum = totals
    entry_new = adamw(entry_weights, entry_momentum, entry_variance, entry_sum, D ** (-0.5))
    temporal_new = adamw(
        temporal_weights, temporal_momentum, temporal_variance, temporal_sum, (D // 2) ** (-0.5)
    )
    spatial_new = adamw(
        spatial_weights,
        spatial_momentum,
        spatial_variance,
        spatial_sum,
        (3 * D // PATCHES) ** (-0.5),
    )
    widen_new = adamw(widen_weights, widen_momentum, widen_variance, widen_sum, D ** (-0.5))
    narrow_new = adamw(narrow_weights, narrow_momentum, narrow_variance, narrow_sum, HID ** (-0.5))
    affine_new = adamw(norm_affine, affine_momentum, affine_variance, affine_sum, 0.5)
    return (
        result,
        input_gradient,
        entry_new[0],
        entry_new[1],
        entry_new[2],
        temporal_new[0],
        temporal_new[1],
        temporal_new[2],
        spatial_new[0],
        spatial_new[1],
        spatial_new[2],
        widen_new[0],
        widen_new[1],
        widen_new[2],
        narrow_new[0],
        narrow_new[1],
        narrow_new[2],
        affine_new[0],
        affine_new[1],
        affine_new[2][:, 0:2],
        affine_new[2][:, 2],
    )


def solution(mesh):
    return jax.shard_map(
        on_device,
        mesh=mesh,
        in_specs=(
            P("clip", "tok", None, None),
            P("clip", "tok", None, None),
            P(("clip", "tok"), None),
            P(("clip", "tok"), None),
            P(("clip", "tok"), None),
            P(("clip", "tok"), None),
            P(("clip", "tok"), None),
            P(("clip", "tok"), None),
            P(("clip", "tok"), None),
            P(("clip", "tok"), None),
            P(("clip", "tok"), None),
            P(("clip", "tok"), None),
            P(("clip", "tok"), None),
            P(("clip", "tok"), None),
            P(("clip", "tok"), None),
            P(("clip", "tok"), None),
            P(("clip", "tok"), None),
            P(None, None, ("clip", "tok")),
            P(None, None, ("clip", "tok")),
            P(None, None, ("clip", "tok")),
        ),
        out_specs=(
            P("clip", "tok", None, None),
            P("clip", "tok", None, None),
            P(("clip", "tok"), None),
            P(("clip", "tok"), None),
            P(("clip", "tok"), None),
            P(("clip", "tok"), None),
            P(("clip", "tok"), None),
            P(("clip", "tok"), None),
            P(("clip", "tok"), None),
            P(("clip", "tok"), None),
            P(("clip", "tok"), None),
            P(("clip", "tok"), None),
            P(("clip", "tok"), None),
            P(("clip", "tok"), None),
            P(("clip", "tok"), None),
            P(("clip", "tok"), None),
            P(("clip", "tok"), None),
            P(None, None, ("clip", "tok")),
            P(None, None, ("clip", "tok")),
            P(None, None, ("clip", "tok")),
            P(None, ("clip", "tok")),
        ),
        check_vma=False,
    )
```

profile of v0, /device:TPU:0, one launch (start us, length us, event | category | flops | bytes accessed | tf_op | source)
XLA Modules:
  0.0 1481.5 jit_solution(14375215329026973542)
XLA Ops:
  21.1 79.3 %all_gather.36 = bf16[2,3,768]{1,0,2:T(2,128)(2,1)S(1)} all-gather(bf16[2,3,24]{1,0,2:T(2,128)(2,1)S(1)} %copy.403), channel_id=1, replica_groups=mesh['clip'=8,'tok'=4] {'clip','tok'}, dimensions={2}, use_global_device_ids=true | all-gather | bytes 9504 | tf_op jit(solution)/shard_map/all_gather | solution.py:101
  100.7 13.2 slice_reduce_fusion.7
  123.9 25.8 %all-gather.11.cloned.1.call-done = bf16[27648,128]{1,0:T(8,128)(2,1)} async-done(((bf16[864,128]{1,0:T(8,128)(2,1)}), bf16[27648,128]{1,0:T(8,128)(2,1)}) %all-gather.11.cloned.1.call-update) | async-done | bytes 7077904 | tf_op jit(solution)/shard_map/all_gather | solution.py:96
  154.3 7.6 reshape.1138
  177.2 17.2 %fusion.260 = (f32[49,12,8]{2,1,0:T(8,128)S(1)}, f32[49,12,8,8]{2,3,1,0:T(8,128)S(1)}) fusion(f32[49,12,8,8]{2,3,1,0:T(8,128)S(1)} %fusion.119), kind=kOutput, calls=%fused_computation.406 | output fusion | flops 150535 | bytes 319872 | tf_op jit(solution)/shard_map/sub | solution.py:67
  211.5 63.5 %all-gather.17.cloned.1.call-done = bf16[18432,128]{1,0:T(8,128)(2,1)} async-done(((bf16[576,128]{1,0:T(8,128)(2,1)}), bf16[18432,128]{1,0:T(8,128)(2,1)}) %all-gather.17.cloned.1.call-update) | async-done | bytes 4718608 | tf_op jit(solution)/shard_map/all_gather | solution.py:99
  275.0 8.2 reshape.1143
  283.2 57.4 %all-gather.19.cloned.1.call-done = bf16[18432,128]{1,0:T(8,128)(2,1)} async-done(((bf16[576,128]{1,0:T(8,128)(2,1)}), bf16[18432,128]{1,0:T(8,128)(2,1)}) %all-gather.19.cloned.1.call-update) | async-done | bytes 4718608 | tf_op jit(solution)/shard_map/all_gather | solution.py:100
  340.6 9.3 reshape.1144
  379.0 25.9 %fusion.96 = bf16[1,2,196,768]{3,2,1,0:T(8,128)(2,1)} fusion(f32[1,2,196,768]{3,2,1,0:T(8,128)S(1)} %get-tuple-element.230, bf16[3072,768,1]{1,0,2:T(8,128)(2,1)S(1)} %bitcast.352, f32[2,196,3072]{2,1,0:T(8,128)S(1)} %get-tuple-element.231, u8[196,3072]{1,0:T(8,128)(4,1)S(1)} %get-tuple-element.164, u8[196,3072]{1,0:T(8,128)(4,1)S(1)} %get-tuple-element.163), kind=kOutput, calls=%fused_computation.165 | convolution fusion | flops 1934585856 | bytes 12546048 | tf_op jit(solution)/shard_map/cfpa,ab->cfpb/dot_general | solution.py:23
  411.5 79.9 %all_gather.43 = bf16[2,3,768]{1,0,2:T(2,128)(2,1)S(1)} all-gather(bf16[2,3,24]{1,0,2:T(2,128)(2,1)S(1)} %copy.430), channel_id=1, replica_groups=mesh['clip'=8,'tok'=4] {'clip','tok'}, dimensions={2}, use_global_device_ids=true | all-gather | bytes 9504 | tf_op jit(solution)/shard_map/all_gather | solution.py:101
  492.4 12.6 slice_reduce_fusion.1
  513.3 27.3 %all-gather.23.cloned.1.call-done = bf16[27648,128]{1,0:T(8,128)(2,1)} async-done(((bf16[864,128]{1,0:T(8,128)(2,1)}), bf16[27648,128]{1,0:T(8,128)(2,1)}) %all-gather.23.cloned.1.call-update) | async-done | bytes 7077904 | tf_op jit(solution)/shard_map/all_gather | solution.py:96
  545.1 7.6 reshape.1146
  584.8 13.4 all-gather.27.cloned.1.call-done
  601.5 67.5 %all-gather.29.cloned.1.call-done = bf16[18432,128]{1,0:T(8,128)(2,1)} async-done(((bf16[576,128]{1,0:T(8,128)(2,1)}), bf16[18432,128]{1,0:T(8,128)(2,1)}) %all-gather.29.cloned.1.call-update) | async-done | bytes 4718608 | tf_op jit(solution)/shard_map/all_gather | solution.py:99
  669.0 8.2 reshape.1151
  677.3 57.4 %all-gather.21.cloned.1.call-done = bf16[18432,128]{1,0:T(8,128)(2,1)} async-done(((bf16[576,128]{1,0:T(8,128)(2,1)}), bf16[18432,128]{1,0:T(8,128)(2,1)}) %all-gather.21.cloned.1.call-update) | async-done | bytes 4718608 | tf_op jit(solution)/shard_map/all_gather | solution.py:100
  734.6 9.2 reshape.1145
  809.8 11.1 all-to-all-done.4
  834.6 16.7 %convolution_bitcast_fusion = f32[3072,768]{1,0:T(8,128)} fusion(f32[2,196,3072]{2,1,0:T(8,128)} %copy-done.74, u8[196,3072]{1,0:T(8,128)(4,1)S(1)} %copy-done.76, u8[196,3072]{1,0:T(8,128)(4,1)S(1)} %copy-done.75, bf16[2,196,768]{2,0,1:T(2,128)(2,1)S(1)} %bitcast.369), kind=kOutput, calls=%fused_computation.6 | convolution fusion | flops 1933983744 | bytes 16060416 | tf_op jit(solution)/shard_map/cfpa,cfpb->ab/dot_general | solution.py:31
  851.4 10.8 reshape.1127
  863.5 7.0 convolution_bitcast_fusion.1
  870.4 10.9 reshape.1126
  882.6 7.0 convolution_bitcast_fusion.3
  915.2 11.0 pad_maximum_fusion
  926.2 15.6 %reshape.1123 = f32[27648,128]{1,0:T(8,128)} reshape(f32[2,768,2304]{2,1,0:T(8,128)} %pad_maximum_fusion) | data formatting | bytes 28311552 | tf_op jit(solution)/shard_map/reshape | solution.py:247
  953.4 42.9 %all-reduce = f32[2,3,768]{2,1,0:T(4,128)S(1)} all-reduce(f32[2,3,768]{2,1,0:T(4,128)S(1)} %pad_maximum_fusion.4), channel_id=7, replica_groups=mesh['clip'=8,'tok'=4] {'clip','tok'}, use_global_device_ids=true, to_apply=%region_39.0.clone | all-reduce | flops 4608 | bytes 36864
  1002.8 20.0 %reduce-scatter.9.cloned.1.call-done = f32[288,128]{1,0:T(8,128)} async-done(((f32[9216,128]{1,0:T(8,128)}), f32[288,128]{1,0:T(8,128)}) %reduce-scatter.9.cloned.1.call-update) | async-done | bytes 147472 | tf_op jit(solution)/shard_map/reduce_scatter | solution.py:256
  1024.6 138.9 %reduce-scatter.15.cloned.1.call-done = f32[576,128]{1,0:T(8,128)} async-done(((f32[18432,128]{1,0:T(8,128)}), f32[576,128]{1,0:T(8,128)}) %reduce-scatter.15.cloned.1.call-update) | async-done | bytes 294928 | tf_op jit(solution)/shard_map/reduce_scatter | solution.py:259
  1165.5 139.4 %reduce-scatter.13.cloned.1.call-done = f32[576,128]{1,0:T(8,128)} async-done(((f32[18432,128]{1,0:T(8,128)}), f32[576,128]{1,0:T(8,128)}) %reduce-scatter.13.cloned.1.call-update) | async-done | bytes 294928 | tf_op jit(solution)/shard_map/reduce_scatter | solution.py:258
  1306.9 165.5 %reduce-scatter.7.cloned.1.call-done = f32[864,128]{1,0:T(8,128)} async-done(((f32[27648,128]{1,0:T(8,128)}), f32[864,128]{1,0:T(8,128)}) %reduce-scatter.7.cloned.1.call-update) | async-done | bytes 442384 | tf_op jit(solution)/shard_map/reduce_scatter | solution.py:255
  (388 shorter events, 278.5 us)
Async XLA Ops:
  7.2 111.2 %all-gather.13.cloned.1.call-start = ((), (), s32[]{:S(2)}) async-start(), calls=%async_computation.12 | async-start | bytes 2433024 | tf_op jit(solution)/shard_map/all_gather | solution.py:97
  8.9 140.9 %all-gather.11.cloned.1.call-start = ((), (), s32[]{:S(2)}) async-start(), calls=%async_computation.11 | async-start | bytes 7299072 | tf_op jit(solution)/shard_map/all_gather | solution.py:96
  10.7 197.5 %all-gather.15.cloned.1.call-start = ((), (), s32[]{:S(2)}) async-start(), calls=%async_computation.13 | async-start | bytes 1216512 | tf_op jit(solution)/shard_map/all_gather | solution.py:98
  12.3 262.7 %all-gather.17.cloned.1.call-start = ((), (), s32[]{:S(2)}) async-start(), calls=%async_computation.14 | async-start | bytes 4866048 | tf_op jit(solution)/shard_map/all_gather | solution.py:99
  14.0 100.0 %all-to-all-start = ((bf16[1,2,196,768]{3,1,0,2:T(2,128)(2,1)}), bf16[1,2,196,768]{3,1,0,2:T(2,128)(2,1)S(1)}, u32[]{:S(2)}, u32[]{:S(2)}) async-start(bf16[1,2,196,768]{3,1,0,2:T(2,128)(2,1)} %bitcast), calls=%async_computation | async-start | bytes 1204224 | tf_op jit(solution)/shard_map/all_to_all | solution.py:117
  20.3 320.3 %all-gather.19.cloned.1.call-start = ((), (), s32[]{:S(2)}) async-start(), calls=%async_computation.15 | async-start | bytes 4866048 | tf_op jit(solution)/shard_map/all_gather | solution.py:100
  203.9 151.2 %all-to-all-start.1 = ((bf16[1,8,49,768]{3,2,0,1:T(8,128)(2,1)}), bf16[1,8,49,768]{3,2,0,1:T(8,128)(2,1)}, u32[]{:S(2)}, u32[]{:S(2)}) async-start(bf16[1,8,49,768]{3,2,0,1:T(8,128)(2,1)} %fusion.104), calls=%async_computation.1 | async-start | bytes 1376256 | tf_op jit(solution)/shard_map/all_to_all | solution.py:126
  208.1 299.7 %all-gather.25.cloned.1.call-start = ((), (), s32[]{:S(2)}) async-start(), calls=%async_computation.18 | async-start | bytes 2433024 | tf_op jit(solution)/shard_map/all_gather | solution.py:97
  404.9 86.9 %copy-start.28 = (f32[576,128]{1,0:T(8,128)S(1)}, f32[576,128]{1,0:T(8,128)}, u32[]{:S(2)}) copy-start(f32[576,128]{1,0:T(8,128)} %param.34) | copy-start | bytes 884740
  405.5 135.0 %all-gather.23.cloned.1.call-start = ((), (), s32[]{:S(2)}) async-start(), calls=%async_computation.17 | async-start | bytes 7299072 | tf_op jit(solution)/shard_map/all_gather | solution.py:96
  406.3 191.9 %all-gather.27.cloned.1.call-start = ((), (), s32[]{:S(2)}) async-start(), calls=%async_computation.19 | async-start | bytes 1216512 | tf_op jit(solution)/shard_map/all_gather | solution.py:98
  407.1 261.9 %all-gather.29.cloned.1.call-start = ((), (), s32[]{:S(2)}) async-start(), calls=%async_computation.20 | async-start | bytes 4866048 | tf_op jit(solution)/shard_map/all_gather | solution.py:99
  407.9 97.2 %all-to-all-start.2 = ((bf16[1,2,196,768]{3,1,0,2:T(2,128)(2,1)}), bf16[1,2,196,768]{3,1,0,2:T(2,128)(2,1)S(1)}, u32[]{:S(2)}, u32[]{:S(2)}) async-start(bf16[1,2,196,768]{3,1,0,2:T(2,128)(2,1)} %bitcast.27), calls=%async_computation.2 | async-start | bytes 1204224 | tf_op jit(solution)/shard_map/all_to_all | solution.py:117
  411.4 323.3 %all-gather.21.cloned.1.call-start = ((), (), s32[]{:S(2)}) async-start(), calls=%async_computation.16 | async-start | bytes 4866048 | tf_op jit(solution)/shard_map/all_gather | solution.py:100
  580.6 168.5 %all-to-all-start.3 = ((bf16[1,8,49,768]{3,2,0,1:T(8,128)(2,1)}), bf16[1,8,49,768]{3,2,0,1:T(8,128)(2,1)}, u32[]{:S(2)}, u32[]{:S(2)}) async-start(bf16[1,8,49,768]{3,2,0,1:T(8,128)(2,1)} %fusion.105), calls=%async_computation.3 | async-start | bytes 1376256 | tf_op jit(solution)/shard_map/all_to_all | solution.py:126
  799.8 21.1 %all-to-all-start.4 = ((bf16[1,2,196,768]{3,1,0,2:T(2,128)(2,1)}), bf16[1,2,196,768]{3,1,0,2:T(2,128)(2,1)}, u32[]{:S(2)}, u32[]{:S(2)}) async-start(bf16[1,2,196,768]{3,1,0,2:T(2,128)(2,1)} %copy.453), calls=%async_computation.4 | async-start | bytes 1204224 | tf_op jit(solution)/shard_map/all_to_all | solution.py:228
  804.0 197.2 %reduce-scatter.11.cloned.1.call-start = ((), (), s32[]{:S(2)}) async-start(), calls=%async_computation.23 | async-start | bytes 2433024 | tf_op jit(solution)/shard_map/reduce_scatter | solution.py:257
  809.7 213.1 %reduce-scatter.9.cloned.1.call-start = ((), (), s32[]{:S(2)}) async-start(), calls=%async_computation.22 | async-start | bytes 4866048 | tf_op jit(solution)/shard_map/reduce_scatter | solution.py:256
  833.2 330.3 %reduce-scatter.15.cloned.1.call-start = ((), (), s32[]{:S(2)}) async-start(), calls=%async_computation.25 | async-start | bytes 9732096 | tf_op jit(solution)/shard_map/reduce_scatter | solution.py:259
  862.2 442.7 %reduce-scatter.13.cloned.1.call-start = ((), (), s32[]{:S(2)}) async-start(), calls=%async_computation.24 | async-start | bytes 9732096 | tf_op jit(solution)/shard_map/reduce_scatter | solution.py:258
  881.4 591.0 %reduce-scatter.7.cloned.1.call-start = ((), (), s32[]{:S(2)}) async-start(), calls=%async_computation.21 | async-start | bytes 14598144 | tf_op jit(solution)/shard_map/reduce_scatter | solution.py:255
  948.4 50.8 %copy-start.15 = (f32[1,2,196,768]{3,2,1,0:T(8,128)S(1)}, f32[1,2,196,768]{3,2,1,0:T(8,128)}, u32[]{:S(2)}) copy-start(f32[1,2,196,768]{3,2,1,0:T(8,128)} %get-tuple-element.208) | copy-start | bytes 3612676
  948.4 50.4 %all-to-all-start.5 = ((bf16[1,8,49,768]{3,2,0,1:T(8,128)(2,1)}), bf16[1,8,49,768]{3,2,0,1:T(8,128)(2,1)S(1)}, u32[]{:S(2)}, u32[]{:S(2)}) async-start(bf16[1,8,49,768]{3,2,0,1:T(8,128)(2,1)} %fusion.131), calls=%async_computation.5 | async-start | bytes 1376256 | tf_op jit(solution)/shard_map/all_to_all | solution.py:242
  999.4 164.1 %copy-start.29 = (f32[576,128]{1,0:T(8,128)S(1)}, f32[576,128]{1,0:T(8,128)}, u32[]{:S(2)}) copy-start(f32[576,128]{1,0:T(8,128)} %param.34) | copy-start | bytes 884740
  999.4 164.1 %copy-start.49 = (f32[576,128]{1,0:T(8,128)S(1)}, f32[576,128]{1,0:T(8,128)}, u32[]{:S(2)}) copy-start(f32[576,128]{1,0:T(8,128)} %param.35) | copy-start | bytes 884740
  999.5 164.0 %copy-start.50 = (f32[576,128]{1,0:T(8,128)S(1)}, f32[576,128]{1,0:T(8,128)}, u32[]{:S(2)}) copy-start(f32[576,128]{1,0:T(8,128)} %param.36) | copy-start | bytes 884740
  1001.1 303.8 %copy-start.31 = (f32[576,128]{1,0:T(8,128)S(1)}, f32[576,128]{1,0:T(8,128)}, u32[]{:S(2)}) copy-start(f32[576,128]{1,0:T(8,128)} %param.31) | copy-start | bytes 884740
  1001.1 303.8 %copy-start.51 = (f32[576,128]{1,0:T(8,128)S(1)}, f32[576,128]{1,0:T(8,128)}, u32[]{:S(2)}) copy-start(f32[576,128]{1,0:T(8,128)} %param.32) | copy-start | bytes 884740
  1001.1 303.8 %copy-start.52 = (f32[576,128]{1,0:T(8,128)S(1)}, f32[576,128]{1,0:T(8,128)}, u32[]{:S(2)}) copy-start(f32[576,128]{1,0:T(8,128)} %param.33) | copy-start | bytes 884740
  1002.8 469.6 %copy-start.18 = (f32[864,128]{1,0:T(8,128)S(1)}, f32[864,128]{1,0:T(8,128)}, u32[]{:S(2)}) copy-start(f32[864,128]{1,0:T(8,128)} %param.22) | copy-start | bytes 1327108
  1002.8 469.6 %copy-start.47 = (f32[864,128]{1,0:T(8,128)S(1)}, f32[864,128]{1,0:T(8,128)}, u32[]{:S(2)}) copy-start(f32[864,128]{1,0:T(8,128)} %param.23) | copy-start | bytes 1327108
  1002.8 469.6 %copy-start.48 = (f32[864,128]{1,0:T(8,128)S(1)}, f32[864,128]{1,0:T(8,128)}, u32[]{:S(2)}) copy-start(f32[864,128]{1,0:T(8,128)} %param.24) | copy-start | bytes 1327108
  (76 other events, 552.6 us)
Sparse Core Ops, SparseCore 0:
  11.4 63.4 all-gather.12
  78.3 71.4 all-gather.10
  153.1 52.7 all-gather.14
  209.1 65.8 all-gather.16
  278.2 62.3 all-gather.18
  405.7 59.9 all-gather.24
  469.0 71.5 all-gather.22
  544.0 54.1 all-gather.26
  601.6 67.4 all-gather.28
  672.3 62.3 all-gather.20
  810.1 99.4 reduce-scatter.10
  915.8 106.9 reduce-scatter.8
  1028.7 134.7 reduce-scatter.14
  1170.3 134.5 reduce-scatter.12
  1310.7 161.6 reduce-scatter.6
where the time goes:
time: 1490 us; the launch traced here: 1480 us
  waiting for transfers between devices  787 us (53%)
  local copies, waits for them, and re-layouts  234 us (16%)
  blocking collectives  202 us (14%)
  matrix products  140 us (9%)
  other arithmetic  75.8 us (5%)
  starting transfers between devices  26.8 us (2%)
  between operations  15.6 us (1%)
    reduce_scatter x1, waiting for transfers between devices, on_device(): lax.psum_scatter(members[0], ('clip', 'tok'), scatter_dimension=0, tiled=...  166 us
    all_gather x2, blocking collectives, collect(): lax.all_gather(masters[5].astype(jnp.bfloat16), ('clip', 'tok'), axis=2,...  159 us
    reduce_scatter x1, waiting for transfers between devices, on_device(): lax.psum_scatter(members[3], ('clip', 'tok'), scatter_dimension=0, tiled=...  139 us
    reduce_scatter x1, waiting for transfers between devices, on_device(): lax.psum_scatter(members[4], ('clip', 'tok'), scatter_dimension=0, tiled=...  139 us
    all_gather x2, waiting for transfers between devices, collect(): lax.all_gather(masters[3].astype(jnp.bfloat16), ('clip', 'tok'), axis=0,...  131 us
    all_gather x2, waiting for transfers between devices, collect(): lax.all_gather(masters[4].astype(jnp.bfloat16), ('clip', 'tok'), axis=0,...  115 us
    dot_general x12, matrix products, project(): jnp.einsum('cfpa,ab->cfpb', inputs, weight, preferred_element_type=jnp.fl...  59.9 us
    all_gather x2, waiting for transfers between devices, collect(): lax.all_gather(masters[0].astype(jnp.bfloat16), ('clip', 'tok'), axis=0,...  53.1 us
  transfers between devices with their start and end apart: 21, of which 12 were waited for; matrix products, arithmetic and copies ran while one was open for 23% of the time, Pallas kernels for 0%

commit v1 on v0

--- a/solution.py
+++ b/solution.py
@@ -1,6 +1,9 @@
+import functools
 import jax
 import jax.numpy as jnp
 from jax import lax
+from jax.experimental import pallas as pl
+from jax.experimental.pallas import tpu as pltpu
 from jax.sharding import PartitionSpec as P
 
 D = 768
@@ -91,27 +94,443 @@
     return stacked.reshape(stacked.shape[:-3] + (3 * HEADS * HEAD_DIM,)).astype(jnp.bfloat16)
 
 
-def collect(masters):
-    gathered = (
-        lax.all_gather(masters[0].astype(jnp.bfloat16), ("clip", "tok"), axis=0, tiled=True),
-        lax.all_gather(masters[1].astype(jnp.bfloat16), ("clip", "tok"), axis=0, tiled=True),
-        lax.all_gather(masters[2].astype(jnp.bfloat16), ("clip", "tok"), axis=0, tiled=True),
-        lax.all_gather(masters[3].astype(jnp.bfloat16), ("clip", "tok"), axis=0, tiled=True),
-        lax.all_gather(masters[4].astype(jnp.bfloat16), ("clip", "tok"), axis=0, tiled=True),
-        lax.all_gather(masters[5].astype(jnp.bfloat16), ("clip", "tok"), axis=2, tiled=True),
-    )
+MESH = pl.DeviceIdType.MESH
+TOK = 4
+
+
+def spot():
+    clip = lax.axis_index("clip")
+    return clip // 4, (clip // 2) % 2, clip % 2, lax.axis_index("tok")
+
+
+def clip_of(y, x, core):
+    return (y * 2 + x) * 2 + core
+
+
+def greet(ny):
+    y, x, core, t = spot()
+    barrier = pltpu.get_barrier_semaphore()
+
+    def tell(clip, tok):
+        pl.semaphore_signal(barrier, inc=1, device_id=(clip, tok), device_id_type=MESH)
+
+    tell(clip_of(y, x, 1 - core), t)
+    tell(clip_of(y, 1 - x, core), t)
+    for far in range(1, ny):
+        tell(clip_of((y + far) % ny, x, core), t)
+    for far in range(1, TOK):
+        tell(clip_of(y, x, core), (t + far) % TOK)
+    pl.semaphore_wait(barrier, 2 + (ny - 1) + (TOK - 1))
+
+
+def gather_kernel(ny, count, *refs):
+    owned, full = refs[:count], refs[count : 2 * count]
+    local, got, got_late, sent_z, sent_x, sent_y, relay_x, relay_y, sent_c = refs[2 * count :]
+    y, x, core, t = spot()
+    greet(ny)
+    me = clip_of(y, x, core) * TOK + t
+
+    def slot(y_at, x_at, t_at):
+        return clip_of(y_at, x_at, core) * TOK + t_at
+
+    def send(k, at, sem, to, tok, half=None, source=None):
+        width = full[k].shape[2]
+        place = full[k].at[at]
+        if half is not None:
+            place = full[k].at[at, :, pl.ds(half * (width // 2), width // 2)]
+        copy = pltpu.make_async_remote_copy(
+            src_ref=place if source is None else source,
+            dst_ref=place,
+            send_sem=sem,
+            recv_sem=(got_late if half == 1 else got).at[k, at],
+            device_id=(to, tok),
+            device_id_type=MESH,
+        )
+        return copy
+
+    started = []
+
+    def go(copy):
+        copy.start()
+        started.append(copy)
+
+    def arrive(k, at, half=None):
+        width = full[k].shape[2]
+        place = full[k].at[at]
+        if half is not None:
+            place = full[k].at[at, :, pl.ds(half * (width // 2), width // 2)]
+        pltpu.make_async_copy(place, place, (got_late if half == 1 else got).at[k, at]).wait()
+
+    def to_core(k, at, number, source=None):
+        go(send(k, at, sent_c.at[k, number], clip_of(y, x, 1 - core), t, source=source))
+
+    def spread(k, j, source=None):
+        at = slot(y, x, (t + j) % TOK)
+        go(send(k, at, sent_x.at[k, j], clip_of(y, 1 - x, core), t, source=source))
+        for far in range(1, ny):
+            go(send(k, at, sent_y.at[k, j * ny + far], clip_of((y + far) % ny, x, core), t, source=source))
+        to_core(k, at, j, source=source)
+
+    splits = [full[k].shape[2] % 256 == 0 for k in range(count)]
+
+    def crossing(k, j):
+        tok = (t + j) % TOK
+        from_x = slot(y, 1 - x, tok)
+        arrive(k, from_x)
+        for far in range(1, ny):
+            if splits[k]:
+                go(send(k, from_x, relay_y.at[k, j * ny + far], clip_of((y + far) % ny, x, core), t, half=1))
+        to_core(k, from_x, 4 + j)
+        for far in range(1, ny):
+            from_y = slot((y + far) % ny, x, tok)
+            arrive(k, from_y)
+            go(
+                send(
+                    k,
+                    from_y,
+                    relay_x.at[k, j * ny + far],
+                    clip_of(y, 1 - x, core),
+                    t,
+                    half=0 if splits[k] else None,
+                )
+            )
+            to_core(k, from_y, 8 + (far - 1) * 8 + j)
+
+    def corner(k, j):
+        tok = (t + j) % TOK
+        for far in range(1, ny):
+            at = slot((y + far) % ny, 1 - x, tok)
+            if splits[k]:
+                arrive(k, at, 0)
+                arrive(k, at, 1)
+            else:
+                arrive(k, at)
+            to_core(k, at, 8 + (far - 1) * 8 + 4 + j)
+
+    kept = []
+    for k in range(count):
+        own = pltpu.make_async_copy(owned[k], full[k].at[me], local.at[k])
+        own.start()
+        kept.append(own)
+        for far in range(1, TOK):
+            go(send(k, me, sent_z.at[k, far], clip_of(y, x, core), (t + far) % TOK, source=owned[k]))
+        spread(k, 0, source=owned[k])
+    steps = [(k, j) for k in range(count) for j in range(TOK)]
+    for n in range(len(steps) + 2):
+        if n < len(steps) and steps[n][1] > 0:
+            k, j = steps[n]
+            arrive(k, slot(y, x, (t + j) % TOK))
+            spread(k, j)
+        if 1 <= n < len(steps) + 1:
+            crossing(*steps[n - 1])
+        if n >= 2:
+            corner(*steps[n - 2])
+    for k in range(count):
+        for at in range(2 * ny):
+            for tok in range(TOK):
+                place = (at * 2 + 1 - core) * TOK + tok
+                arrive(k, place)
+    for own in kept:
+        own.wait()
+    for copy in started:
+        copy.wait_send()
+
+
+def gather_all(owned, clips):
+    ny = clips // 4
+    count = len(owned)
+    devices = clips * TOK
+    dma = pltpu.SemaphoreType.DMA
+    return pl.pallas_call(
+        functools.partial(gather_kernel, ny, count),
+        out_shape=[jax.ShapeDtypeStruct((devices,) + a.shape, a.dtype) for a in owned],
+        in_specs=[pl.BlockSpec(memory_space=pl.ANY)] * count,
+        out_specs=[pl.BlockSpec(memory_space=pl.ANY)] * count,
+        scratch_shapes=[
+            dma((count,)),
+            dma((count, devices)),
+            dma((count, devices)),
+            dma((count, TOK)),
+            dma((count, TOK)),
+            dma((count, TOK * ny)),
+            dma((count, TOK * ny)),
+            dma((count, TOK * ny)),
+            dma((count, 8 * ny)),
+        ],
+        compiler_params=pltpu.CompilerParams(collective_id=0, has_side_effects=True),
+    )(*owned)
+
+
+def scatter_kernel(ny, count, *refs):
+    parts, totals = refs[:count], refs[count : 2 * count]
+    rest = refs[2 * count :]
+    held, core_in, side_in, part_in, z_in = (rest[i * count : (i + 1) * count] for i in range(5))
+    load_sem, c_send, c_recv, d_send, d_recv, s_send, s_recv, z_send, z_recv = rest[5 * count :]
+    y, x, core, t = spot()
+    greet(ny)
+    started = []
+
+    def go(copy):
+        copy.start()
+        started.append(copy)
+        return copy
+
+    groups = [(dy, dx) for dy in range(1, ny) for dx in (1,)] + [(0, 1)] + [(dy, 0) for dy in range(1, ny)] + [(0, 0)]
+    number = {pair: i for i, pair in enumerate(groups)}
+
+    def absolute(pair):
+        return (y + pair[0]) % ny, (x + pair[1]) % 2
+
+    loads, cores = {}, {}
+
+    def begin(k):
+        for pair in groups:
+            i = number[pair]
+            ya, xa = absolute(pair)
+            load = pltpu.make_async_copy(
+                parts[k].at[pl.ds(clip_of(ya, xa, core) * TOK, TOK)], held[k].at[i], load_sem.at[k, i]
+            )
+            load.start()
+            loads[k, pair] = load
+            cores[k, pair] = go(
+                pltpu.make_async_remote_copy(
+                    src_ref=parts[k].at[pl.ds(clip_of(ya, xa, 1 - core) * TOK, TOK)],
+                    dst_ref=core_in[k].at[i],
+                    send_sem=c_send.at[k, i],
+                    recv_sem=c_recv.at[k, i],
+                    device_id=(clip_of(y, x, 1 - core), t),
+                    device_id_type=MESH,
+                )
+            )
+
+    def ready(k, pair):
+        loads[k, pair].wait()
+        cores[k, pair].wait_recv()
+
+    def add_into(k, i, pieces):
+        width = held[k].shape[3]
+        cuts = sorted({0, width} | {c for _, a, b in pieces for c in (a, b)})
+        for a, b in zip(cuts[:-1], cuts[1:]):
+            live = [(make, lo) for make, lo, hi in pieces if lo <= a and b <= hi]
+
+            def one(j, carry, a=a, b=b, live=live):
+                total = held[k][i, j, :, a:b].astype(jnp.float32)
+                for make, lo in live:
+                    total = total + make(j, a - lo, b - lo).astype(jnp.float32)
+                held[k][i, j, :, a:b] = total.astype(held[k].dtype)
+                return carry
+
+            lax.fori_loop(0, TOK, one, 0)
+
+    def cut(k):
+        width = held[k].shape[3]
+        return width // 2 if width % 256 == 0 else width
+
+    firsts, seconds, lasts = {}, {}, {}
+
+    def step1(k):
+        width, mid = held[k].shape[3], cut(k)
+        for dy in range(1, ny):
+            i = number[dy, 1]
+            ready(k, (dy, 1))
+            add_into(k, i, [(lambda j, a, b, i=i: core_in[k][i, j, :, a:b], 0, width)])
+            firsts[k, dy, 0] = go(
+                pltpu.make_async_remote_copy(
+                    src_ref=held[k].at[i, :, :, pl.ds(0, mid)],
+                    dst_ref=side_in[k].at[dy - 1, :, :, pl.ds(0, mid)],
+                    send_sem=d_send.at[k, dy, 0],
+                    recv_sem=d_recv.at[k, dy, 0],
+                    device_id=(clip_of(y, 1 - x, core), t),
+                    device_id_type=MESH,
+                )
+            )
+            if mid < width:
+                firsts[k, dy, 1] = go(
+                    pltpu.make_async_remote_copy(
+                        src_ref=held[k].at[i, :, :, pl.ds(mid, width - mid)],
+                        dst_ref=side_in[k].at[dy - 1, :, :, pl.ds(mid, width - mid)],
+                        send_sem=d_send.at[k, dy, 1],
+                        recv_sem=d_recv.at[k, dy, 1],
+                        device_id=(clip_of((y + dy) % ny, x, core), t),
+                        device_id_type=MESH,
+                    )
+                )
+
+    def step2(k):
+        width, mid = held[k].shape[3], cut(k)
+        for dy in range(1, ny):
+            i = number[dy, 0]
+            ready(k, (dy, 0))
+            firsts[k, dy, 0].wait_recv()
+            add_into(
+                k,
+                i,
+                [
+                    (lambda j, a, b, i=i: core_in[k][i, j, :, a:b], 0, width),
+                    (lambda j, a, b, dy=dy: side_in[k][dy - 1, j, :, a:b], 0, mid),
+                ],
+            )
+            seconds[k, dy] = go(
+                pltpu.make_async_remote_copy(
+                    src_ref=held[k].at[i],
+                    dst_ref=part_in[k].at[dy],
+                    send_sem=s_send.at[k, dy],
+                    recv_sem=s_recv.at[k, dy],
+                    device_id=(clip_of((y + dy) % ny, x, core), t),
+                    device_id_type=MESH,
+                )
+            )
+        i = number[0, 1]
+        ready(k, (0, 1))
+        pieces = [(lambda j, a, b, i=i: core_in[k][i, j, :, a:b], 0, width)]
+        if mid < width:
+            for dy in range(1, ny):
+                firsts[k, dy, 1].wait_recv()
+                pieces.append(
+                    (lambda j, a, b, dy=dy: side_in[k][dy - 1, j, :, a + mid : b + mid], mid, width)
+                )
+        add_into(k, i, pieces)
+        seconds[k, 0] = go(
+            pltpu.make_async_remote_copy(
+                src_ref=held[k].at[i],
+                dst_ref=part_in[k].at[0],
+                send_sem=s_send.at[k, 0],
+                recv_sem=s_recv.at[k, 0],
+                device_id=(clip_of(y, 1 - x, core), t),
+                device_id_type=MESH,
+            )
+        )
+
+    def step3(k):
+        width = held[k].shape[3]
+        i = number[0, 0]
+        ready(k, (0, 0))
+        for dy in range(ny):
+            seconds[k, dy].wait_recv()
+        pieces = [(lambda j, a, b, i=i: core_in[k][i, j, :, a:b], 0, width)]
+        for dy in range(ny):
+            pieces.append((lambda j, a, b, dy=dy: part_in[k][dy, j, :, a:b], 0, width))
+        add_into(k, i, pieces)
+        for far in range(1, TOK):
+            lasts[k, far] = go(
+                pltpu.make_async_remote_copy(
+                    src_ref=held[k].at[i, (t + far) % TOK],
+                    dst_ref=z_in[k].at[far - 1],
+                    send_sem=z_send.at[k, far],
+                    recv_sem=z_recv.at[k, far],
+                    device_id=(clip_of(y, x, core), (t + far) % TOK),
+                    device_id_type=MESH,
+                )
+            )
+
+    def step4(k):
+        i = number[0, 0]
+        total = held[k][i, t].astype(jnp.float32)
+        for far in range(1, TOK):
+            lasts[k, far].wait_recv()
+            total = total + z_in[k][far - 1].astype(jnp.float32)
+        totals[k][...] = total
+
+    for k in range(count):
+        begin(k)
+    for n in range(count + 3):
+        for shift, step in enumerate((step1, step2, step3, step4)):
+            if 0 <= n - shift < count:
+                step(n - shift)
+    for copy in started:
+        copy.wait_send()
+
+
+def scatter_all(parts, clips):
+    ny = clips // 4
+    count = len(parts)
+    dma = pltpu.SemaphoreType.DMA
+    shapes = [p.shape[1:] for p in parts]
+    held = [pltpu.VMEM((2 * ny, TOK) + s, jnp.bfloat16) for s in shapes]
+    side = [pltpu.VMEM((max(ny - 1, 1), TOK) + s, jnp.bfloat16) for s in shapes]
+    part = [pltpu.VMEM((ny, TOK) + s, jnp.bfloat16) for s in shapes]
+    last = [pltpu.VMEM((TOK - 1,) + s, jnp.bfloat16) for s in shapes]
+    return pl.pallas_call(
+        functools.partial(scatter_kernel, ny, count),
+        out_shape=[jax.ShapeDtypeStruct(s, jnp.float32) for s in shapes],
+        in_specs=[pl.BlockSpec(memory_space=pl.ANY)] * count,
+        out_specs=[pl.BlockSpec(memory_space=pltpu.VMEM)] * count,
+        scratch_shapes=held + held + side + part + last
+        + [
+            dma((count, 2 * ny)),
+            dma((count, 2 * ny)),
+            dma((count, 2 * ny)),
+            dma((count, ny, 2)),
+            dma((count, ny, 2)),
+            dma((count, ny)),
+            dma((count, ny)),
+            dma((count, TOK)),
+            dma((count, TOK)),
+        ],
+        compiler_params=pltpu.CompilerParams(
+            collective_id=1, has_side_effects=True, vmem_limit_bytes=58 * 1024 * 1024
+        ),
+    )(*parts)
+
+
+def as_rows(masters, devices):
+    entry, temporal, spatial, widen, narrow, affine = (m.astype(jnp.bfloat16) for m in masters)
+    each = affine.shape[2]
     return (
-        gathered[0].reshape(2, D, 3 * D),
-        gathered[1].reshape(2, D, D),
-        gathered[2].reshape(D, D),
-        gathered[3].reshape(D, HID),
-        gathered[4].reshape(HID, D),
-        gathered[5],
-    )
-
-
-def forward(frames, masters):
-    weights = collect(masters)
+        entry.reshape(2 * D // devices, 3 * D),
+        temporal.reshape(2 * D // devices, D),
+        spatial.reshape(D // devices, D),
+        widen.reshape(D // devices, HID),
+        narrow.reshape(HID // devices, D),
+        jnp.pad(affine.reshape(6, each), ((0, 10), (0, 128 - each))),
+    )
+
+
+def collect(masters, clips):
+    devices = clips * TOK
+    rows = as_rows(masters, devices)
+    if clips == 8:
+        full = gather_all(rows, clips)
+    else:
+        full = [lax.all_gather(r, ("clip", "tok"), axis=0) for r in rows]
+    each = D // devices
+    affine = full[5][:, :6, :each].transpose(1, 0, 2).reshape(2, 3, D)
+    return (
+        full[0].reshape(2, D, 3 * D),
+        full[1].reshape(2, D, D),
+        full[2].reshape(D, D),
+        full[3].reshape(D, HID),
+        full[4].reshape(HID, D),
+        affine,
+    )
+
+
+def spread_sums(grads, clips):
+    devices = clips * TOK
+    each = D // devices
+    affine = grads[5].reshape(6, devices, each).transpose(1, 0, 2)
+    parts = (
+        grads[0].reshape(devices, 2 * D // devices, 3 * D),
+        grads[1].reshape(devices, 2 * D // devices, D),
+        grads[2].reshape(devices, D // devices, D),
+        grads[3].reshape(devices, D // devices, HID),
+        grads[4].reshape(devices, HID // devices, D),
+        jnp.pad(affine, ((0, 0), (0, 10), (0, 128 - each))),
+    )
+    parts = tuple(p.astype(jnp.bfloat16) for p in parts)
+    if clips == 8:
+        sums = scatter_all(parts, clips)
+    else:
+        sums = [
+            lax.psum_scatter(p, ("clip", "tok"), scatter_dimension=0).astype(jnp.float32)
+            for p in parts
+        ]
+    flat = tuple(s.reshape(-1, 128) for s in sums[:5])
+    return flat + (sums[5][:6, :each].reshape(2, 3, each),)
+
+
+def forward(frames, masters, clips):
+    weights = collect(masters, clips)
     entry, temporal, spatial, widen, narrow, affine = weights
     gains = affine.astype(jnp.float32)
     patchwise = lax.all_to_all(frames, "tok", split_axis=2, concat_axis=1, tiled=True)
@@ -197,9 +616,8 @@
         narrow_weights,
         norm_affine,
     )
-    result, unused = forward(frames, masters)
-    fenced = lax.optimization_barrier((frames, masters, result))
-    again, saved = forward(fenced[0], fenced[1])
+    clips = lax.axis_size("clip")
+    result, saved = forward(frames, masters, clips)
     entry, temporal, spatial, widen, narrow, affine = saved["weights"]
     gains = affine.astype(jnp.float32)
     narrow_grad = weight_sum(saved["activated"], cotangent)
@@ -244,21 +662,14 @@
     )
     input_gradient = dafter_t + dreturned.astype(jnp.float32)
     members = (
-        jnp.stack([entry_grad_t, entry_grad_s]).reshape(-1, 128),
-        jnp.stack([temporal_grad_a, temporal_grad_b]).reshape(-1, 128),
-        spatial_grad.reshape(-1, 128),
-        widen_grad.reshape(-1, 128),
-        narrow_grad.reshape(-1, 128),
+        jnp.stack([entry_grad_t, entry_grad_s]),
+        jnp.stack([temporal_grad_a, temporal_grad_b]),
+        spatial_grad,
+        widen_grad,
+        narrow_grad,
         jnp.stack([jnp.stack([gain_t, gain_s, gain_m]), jnp.stack([shift_t, shift_s, shift_m])]),
     )
-    totals = (
-        lax.psum_scatter(members[0], ("clip", "tok"), scatter_dimension=0, tiled=True),
-        lax.psum_scatter(members[1], ("clip", "tok"), scatter_dimension=0, tiled=True),
-        lax.psum_scatter(members[2], ("clip", "tok"), scatter_dimension=0, tiled=True),
-        lax.psum_scatter(members[3], ("clip", "tok"), scatter_dimension=0, tiled=True),
-        lax.psum_scatter(members[4], ("clip", "tok"), scatter_dimension=0, tiled=True),
-        lax.psum_scatter(members[5], ("clip", "tok"), scatter_dimension=2, tiled=True),
-    )
+    totals = spread_sums(members, clips)
     entry_sum, temporal_sum, spatial_sum, widen_sum, narrow_sum, affine_sum = totals
     entry_new = adamw(entry_weights, entry_momentum, entry_variance, entry_sum, D ** (-0.5))
     temporal_new = adamw(

time: 1490 us -> 513 us (0.34)
  waiting for transfers between devices: 787 us -> 15.4 us
  Pallas kernels: 0 us -> 227 us
  blocking collectives: 202 us -> 0 us
  local copies, waits for them, and re-layouts: 234 us -> 81 us
  matrix products: 140 us -> 95.6 us
  other arithmetic: 75.8 us -> 42.9 us
    reduce_scatter x5 -> x0, waiting for transfers between devices: 464 us -> none  [the longest x1 166 us: on_device(): lax.psum_scatter(members[0], ('clip', 'tok'), scatter_dimension=0, tiled=...]
    all_gather x10 -> x0, waiting for transfers between devices: 312 us -> none  [the longest x2 131 us: collect(): lax.all_gather(masters[3].astype(jnp.bfloat16), ('clip', 'tok'), axis=0,...]
    pallas_call x0 -> x2, Pallas kernels: none -> 227 us  [the longest x1 114 us: gather_all(): pl.pallas_call(functools.partial(gather_kernel, ny, count), out_shape=[ja...]
    all_gather x2 -> x0, blocking collectives: 159 us -> none  [collect(): lax.all_gather(masters[5].astype(jnp.bfloat16), ('clip', 'tok'), axis=2,...]
    reshape x11 -> x14, local copies, waits for them, and re-layouts: 87.9 us -> 8.47 us  [the longest x5 3 us: spread_sums(): flat = tuple((s.reshape(-1, 128) for s in sums[:5]))]
    unnamed x1 -> x0, blocking collectives: 42.9 us -> none
    squeeze x8 -> x0, local copies, waits for them, and re-layouts: 33.1 us -> none  [the longest x2 15.2 us: forward(): heads_t = split_heads(project(lowered_t, entry[0]))]
    dot_general x12 -> x7, matrix products: 59.9 us -> 29.9 us  [project(): jnp.einsum('cfpa,ab->cfpb', inputs, weight, preferred_element_type=jnp.fl...]
  transfers between devices with their start and end apart: 21 -> 4, of which waited for: 12 -> 1; matrix products, arithmetic and copies ran while one was open for 23% -> 16% of each run, Pallas kernels for 0% -> 45%
where the time goes in v1:
time: 513 us; the launch traced here: 505 us
  Pallas kernels  227 us (44%)
  matrix products  95.6 us (19%)
  local copies, waits for them, and re-layouts  81 us (16%)
  other arithmetic  42.9 us (8%)
  starting transfers between devices  41.1 us (8%)
  waiting for transfers between devices  15.4 us (3%)
    pallas_call x1, Pallas kernels, gather_all(): pl.pallas_call(functools.partial(gather_kernel, ny, count), out_shape=[ja...  114 us
    pallas_call x1, Pallas kernels, scatter_all(): pl.pallas_call(functools.partial(scatter_kernel, ny, count), out_shape=[j...  113 us
    dot_general x7, matrix products, project(): jnp.einsum('cfpa,ab->cfpb', inputs, weight, preferred_element_type=jnp.fl...  29.9 us
    dot_general x7, matrix products, weight_sum(): jnp.einsum('cfpa,cfpb->ab', inputs, upstream, preferred_element_type=jnp....  26.8 us
    all_to_all x1, starting transfers between devices, forward(): lax.all_to_all(branch, 'tok', split_axis=1, concat_axis=2, tiled=True)  25.3 us
    dot_general x7, matrix products, project_back(): jnp.einsum('cfpb,ab->cfpa', upstream, weight, preferred_element_type=jnp....  16.7 us
    unnamed x174, local copies, waits for them, and re-layouts  16.4 us
    all_to_all x1, waiting for transfers between devices, forward(): lax.all_to_all(branch, 'tok', split_axis=1, concat_axis=2, tiled=True)  15.4 us
  transfers between devices with their start and end apart: 4, of which 1 were waited for; matrix products, arithmetic and copies ran while one was open for 16% of the time, Pallas kernels for 45%

profile of v1, /device:TPU:0, one launch (start us, length us, event | category | flops | bytes accessed | tf_op | source)
XLA Modules:
  0.0 505.0 jit_solution(10176178361917312911)
XLA Ops:
  0.7 6.5 %all-to-all-start = ((bf16[1,2,196,768]{3,1,0,2:T(2,128)(2,1)}), bf16[1,2,196,768]{3,1,0,2:T(2,128)(2,1)S(1)}, u32[]{:S(2)}, u32[]{:S(2)}) async-start(bf16[1,2,196,768]{3,1,0,2:T(2,128)(2,1)} %bitcast.395), calls=%async_computation | async-start | bytes 1204224 | tf_op jit(solution)/shard_map/all_to_all | solution.py:536
  12.8 113.7 %shard_map.355 = (bf16[32,48,2304]{2,1,0:T(8,128)(2,1)}, bf16[32,48,768]{2,1,0:T(8,128)(2,1)}, bf16[32,24,768]{2,1,0:T(8,128)(2,1)}, bf16[32,24,3072]{2,1,0:T(8,...) custom-call(bf16[48,2304]{1,0:T(8,128)(2,1)} %reshape.814.refs_0_, ...), custom_call_target="tpu_custom_call" | custom-call | tf_op jit(solution)/shard_map/pallas_call | solution.py:244
  126.5 3.3 fusion.167
  130.1 6.4 %fusion.165 = (bf16[16,48,2304]{2,1,0:T(8,128)(2,1)}, bf16[16,48,2304]{2,1,0:T(8,128)(2,1)}) fusion(bf16[32,48,2304]{2,1,0:T(8,128)(2,1)} %get-tuple-element.34), kind=kLoop, calls=%fused_computation.276 | loop fusion | bytes 14155776 | tf_op jit(solution)/shard_map/slice | solution.py:549
  140.9 4.4 reshape.870
  145.4 3.3 fusion.166
  154.2 3.2 convert_element_type.321
  162.0 25.3 %all-to-all-start.1 = ((bf16[1,8,49,768]{3,2,0,1:T(8,128)(2,1)}), bf16[1,8,49,768]{3,2,0,1:T(8,128)(2,1)}, u32[]{:S(2)}, u32[]{:S(2)}) async-start(bf16[1,8,49,768]{3,2,0,1:T(8,128)(2,1)} %fusion.73), calls=%async_computation.1 | async-start | bytes 1376256 | tf_op jit(solution)/shard_map/all_to_all | solution.py:545
  190.9 15.4 %all-to-all-done.1 = bf16[1,8,49,768]{3,2,0,1:T(8,128)(2,1)} async-done(((bf16[1,8,49,768]{3,2,0,1:T(8,128)(2,1)}), bf16[1,8,49,768]{3,2,0,1:T(8,128)(2,1)}, u32[]{:S(2)}, u32[]{:S(2)}) %all-to-all-start.1) | async-done | bytes 602144 | tf_op jit(solution)/shard_map/all_to_all | solution.py:545
  210.3 3.0 convolution_convert_fusion.1
  213.3 4.1 copy.146
  222.2 3.3 fusion.56
  226.7 4.5 fusion.83
  231.3 4.3 fusion.8
  243.7 3.5 fusion.70
  247.3 4.1 multiply_reduce_fusion
  259.4 4.6 fusion.33
  264.0 11.5 %fusion.11 = bf16[3072,2,196]{0,2,1:T(8,128)(2,1)} fusion(f32[2,196,3072]{2,1,0:T(8,128)S(1)} %bitcast.384), kind=kLoop, calls=%fused_computation.19 | loop fusion | flops 78274560 | bytes 7225344 | tf_op jit(solution)/shard_map/convert_element_type | solution.py:555
  278.6 4.2 all-to-all-start.2
  282.8 5.5 %dot_general.166 = bf16[32,96,2,196]{1,0,3,2:T(8,128)(2,1)} reshape(bf16[3072,2,196]{0,2,1:T(8,128)(2,1)} %fusion.11) | data formatting | bytes 4816896 | tf_op jit(solution)/shard_map/cfpa,cfpb->ab/dot_general | solution.py:34
  288.3 15.9 %fusion.65 = bf16[1,2,196,768]{3,2,1,0:T(8,128)(2,1)S(1)} fusion(f32[1,2,196,768]{3,2,1,0:T(8,128)} %copy-done.4, bf16[3072,768,1]{1,0,2:T(8,128)(2,1)} %bitcast.415, f32[2,196,3072]{2,1,0:T(8,128)} %copy-done.19, u8[196,3072]{1,0:T(8,128)(4,1)} %get-tuple-element.109, u8[196,3072]{1,0:T(8,128)(4,1)S(1)} %copy-done.76), kind=kOutput, calls=%fused_computation.120 | convolution fusion | flops 1934585856 | bytes 12546048 | tf_op jit(solution)/shard_map/cfpa,ab->cfpb/dot_general | solution.py:26
  304.2 6.8 %bitcast_convert_fusion.refs_4_ = bf16[32,96,768]{2,1,0:T(8,128)(2,1)} fusion(bf16[32,96,2,196]{1,0,3,2:T(8,128)(2,1)S(1)} %copy-done.6, bf16[2,196,768]{2,0,1:T(2,128)(2,1)S(1)} %bitcast.394), kind=kOutput, calls=%fused_computation | convolution fusion | flops 1852047360 | bytes 7729152 | tf_op jit(solution)/shard_map/cfpa,cfpb->ab/dot_general | solution.py:34
  313.5 3.6 bitcast_convert_fusion.4.refs_2_
  317.1 4.4 bitcast_convert_fusion.1.refs_3_
  327.3 3.0 reshape.871
  342.8 2.9 copy.202
  345.7 5.3 %reshape.872 = bf16[8,49,2304]{2,1,0:T(8,128)(2,1)S(1)} reshape(bf16[1,8,49,3,12,64]{5,4,3,2,1,0:T(8,128)(2,1)} %copy.202) | data formatting | bytes 3612672 | tf_op jit(solution)/shard_map/convert_element_type | solution.py:94
  351.0 3.8 fusion.32
  354.8 2.5 multiply_reduce_fusion.4
  358.7 5.2 %all-to-all-start.3 = ((bf16[1,8,49,768]{3,2,0,1:T(8,128)(2,1)}), bf16[1,8,49,768]{3,2,0,1:T(8,128)(2,1)}, u32[]{:S(2)}, u32[]{:S(2)}) async-start(bf16[1,8,49,768]{3,2,0,1:T(8,128)(2,1)} %fusion.93), calls=%async_computation.3 | async-start | bytes 1376256 | tf_op jit(solution)/shard_map/all_to_all | solution.py:660
  367.5 5.7 %pad_maximum_fusion = bf16[2,768,2304]{2,1,0:T(8,128)(2,1)} fusion(bf16[1,768,2304]{2,1,0:T(8,128)(2,1)S(1)} %copy-done.24, bf16[1,768,2304]{2,1,0:T(8,128)(2,1)} %fusion.32), kind=kLoop, calls=%fused_computation.5 | loop fusion | flops 3538944 | bytes 14155776 | tf_op jit(solution)/shard_map/stack | solution.py:665
  374.9 113.3 %shard_map.356 = (f32[48,2304]{1,0:T(8,128)}, f32[48,768]{1,0:T(8,128)}, f32[24,768]{1,0:T(8,128)}, f32[24,3072]{1,0:T(8,128)}, f32[96,768]{1,0:T(8,128)}, /*index=5*/f32[16,128]{1,0:T(8,128)}) custom-call(bf16[32,48,2304]{2,1,0:T(8,128)(2,1)} %bitcast.372, bf16[32,48,768]{2,1,0:T(8,128)(2,1)} %bitcast.378, ...), custom_call_target="tpu_custom_call" | custom-call | tf_op jit(solution)/shard_map/pallas_call | solution.py:453
  (289 shorter events, 96.6 us)
Async XLA Ops:
  0.7 8.5 %copy-start.47 = (f32[288,128]{1,0:T(8,128)S(1)}, f32[288,128]{1,0:T(8,128)}, u32[]{:S(2)}) copy-start(f32[288,128]{1,0:T(8,128)} %param.25) | copy-start | bytes 442372
  0.7 9.2 %copy-start.53 = (f32[144,128]{1,0:T(8,128)S(1)}, f32[144,128]{1,0:T(8,128)}, u32[]{:S(2)}) copy-start(f32[144,128]{1,0:T(8,128)} %param.28) | copy-start | bytes 221188
  0.7 9.9 %copy-start.34 = (f32[576,128]{1,0:T(8,128)S(1)}, f32[576,128]{1,0:T(8,128)}, u32[]{:S(2)}) copy-start(f32[576,128]{1,0:T(8,128)} %param.31) | copy-start | bytes 884740
  0.7 10.7 %copy-start.36 = (f32[576,128]{1,0:T(8,128)S(1)}, f32[576,128]{1,0:T(8,128)}, u32[]{:S(2)}) copy-start(f32[576,128]{1,0:T(8,128)} %param.34) | copy-start | bytes 884740
  0.7 11.5 %copy-start.66 = (f32[2,3,24]{2,0,1:T(2,128)S(1)}, f32[2,3,24]{2,0,1:T(2,128)}, u32[]{:S(2)}) copy-start(f32[2,3,24]{2,0,1:T(2,128)} %param.37) | copy-start | bytes 1732
  0.7 135.7 %all-to-all-start = ((bf16[1,2,196,768]{3,1,0,2:T(2,128)(2,1)}), bf16[1,2,196,768]{3,1,0,2:T(2,128)(2,1)S(1)}, u32[]{:S(2)}, u32[]{:S(2)}) async-start(bf16[1,2,196,768]{3,1,0,2:T(2,128)(2,1)} %bitcast.395), calls=%async_computation | async-start | bytes 1204224 | tf_op jit(solution)/shard_map/all_to_all | solution.py:536
  130.0 7.3 %copy-start.63 = (f32[768]{0:T(1024)}, f32[768]{0:T(1024)S(1)}, u32[]{:S(2)}) copy-start(f32[768]{0:T(1024)S(1)} %get-tuple-element.127) | copy-start | bytes 9220
  137.0 52.5 %copy-start.57 = (f32[4,2,49]{2,1,0:T(2,128)}, f32[4,2,49]{2,1,0:T(2,128)S(1)}, u32[]{:S(2)}) copy-start(f32[4,2,49]{2,1,0:T(2,128)S(1)} %broadcast_multiply_fusion.2) | copy-start | bytes 4708
  137.3 52.2 %copy-start.61 = (f32[4,2,49]{2,1,0:T(2,128)}, f32[4,2,49]{2,1,0:T(2,128)S(1)}, u32[]{:S(2)}) copy-start(f32[4,2,49]{2,1,0:T(2,128)S(1)} %add_rsqrt_fusion) | copy-start | bytes 4708
  162.0 44.3 %all-to-all-start.1 = ((bf16[1,8,49,768]{3,2,0,1:T(8,128)(2,1)}), bf16[1,8,49,768]{3,2,0,1:T(8,128)(2,1)}, u32[]{:S(2)}, u32[]{:S(2)}) async-start(bf16[1,8,49,768]{3,2,0,1:T(8,128)(2,1)} %fusion.73), calls=%async_computation.1 | async-start | bytes 1376256 | tf_op jit(solution)/shard_map/all_to_all | solution.py:545
  189.6 18.3 %copy-start.30 = (bf16[1,2,196,768]{3,1,2,0:T(2,128)(2,1)S(1)}, bf16[1,2,196,768]{3,1,2,0:T(2,128)(2,1)}, u32[]{:S(2)}) copy-start(bf16[1,2,196,768]{3,1,2,0:T(2,128)(2,1)} %param.20) | copy-start | bytes 1806340
  219.7 7.0 %slice-start.6 = ((s8[4718592]{0:T(1024)(128)(4,1)}), s8[4194304]{0:T(1024)(128)(4,1)S(1)}, s32[]{:S(2)}) async-start(s8[4718592]{0:T(1024)(128)(4,1)} %bitcast.419), calls=%async_computation.10 | async-start | bytes 8388608
  226.3 13.0 %copy-start.4 = (f32[1,2,196,768]{3,2,1,0:T(8,128)}, f32[1,2,196,768]{3,2,1,0:T(8,128)S(1)}, u32[]{:S(2)}) copy-start(f32[1,2,196,768]{3,2,1,0:T(8,128)S(1)} %get-tuple-element.163) | copy-start | bytes 3612676
  243.7 7.7 %slice-start = ((s8[4915200]{0:T(1024)(128)(4,1)}), s8[4194304]{0:T(1024)(128)(4,1)S(1)}, s32[]{:S(2)}) async-start(s8[4915200]{0:T(1024)(128)(4,1)} %bitcast.370), calls=%async_computation.4 | async-start | bytes 8388608
  257.0 7.0 %slice-start.2 = ((s8[4915200]{0:T(1024)(128)(4,1)}), s8[4194304]{0:T(1024)(128)(4,1)S(1)}, s32[]{:S(2)}) async-start(s8[4915200]{0:T(1024)(128)(4,1)} %bitcast.383), calls=%async_computation.6 | async-start | bytes 8388608
  264.0 11.7 %copy-start.10 = (f32[1,2,196,768]{3,2,1,0:T(8,128)S(1)}, f32[1,2,196,768]{3,2,1,0:T(8,128)}, u32[]{:S(2)}) copy-start(f32[1,2,196,768]{3,2,1,0:T(8,128)} %copy-done.9) | copy-start | bytes 3612676
  278.6 42.9 %all-to-all-start.2 = ((bf16[1,2,196,768]{3,1,0,2:T(2,128)(2,1)}), bf16[1,2,196,768]{3,1,0,2:T(2,128)(2,1)}, u32[]{:S(2)}, u32[]{:S(2)}) async-start(bf16[1,2,196,768]{3,1,0,2:T(2,128)(2,1)} %copy.160), calls=%async_computation.2 | async-start | bytes 1204224 | tf_op jit(solution)/shard_map/all_to_all | solution.py:646
  288.3 15.9 %copy-start.6 = (bf16[32,96,2,196]{1,0,3,2:T(8,128)(2,1)S(1)}, bf16[32,96,2,196]{1,0,3,2:T(8,128)(2,1)}, u32[]{:S(2)}) copy-start(bf16[32,96,2,196]{1,0,3,2:T(8,128)(2,1)} %dot_general.166) | copy-start | bytes 7225348
  288.3 15.9 %copy-start.28 = (bf16[1,2,196,768]{3,1,2,0:T(2,128)(2,1)S(1)}, bf16[1,2,196,768]{3,1,2,0:T(2,128)(2,1)}, u32[]{:S(2)}) copy-start(bf16[1,2,196,768]{3,1,2,0:T(2,128)(2,1)} %param.21) | copy-start | bytes 1806340
  304.2 8.1 %copy-start.29 = (bf16[768,2,196]{0,2,1:T(8,128)(2,1)S(1)}, bf16[768,2,196]{0,2,1:T(8,128)(2,1)}, u32[]{:S(2)}) copy-start(bf16[768,2,196]{0,2,1:T(8,128)(2,1)} %get-tuple-element.157) | copy-start | bytes 1806340
  357.4 10.2 %copy-start.24 = (bf16[1,768,2304]{2,1,0:T(8,128)(2,1)S(1)}, bf16[1,768,2304]{2,1,0:T(8,128)(2,1)}, u32[]{:S(2)}) copy-start(bf16[1,768,2304]{2,1,0:T(8,128)(2,1)} %fusion.33) | copy-start | bytes 10616836
  358.7 142.7 %all-to-all-start.3 = ((bf16[1,8,49,768]{3,2,0,1:T(8,128)(2,1)}), bf16[1,8,49,768]{3,2,0,1:T(8,128)(2,1)}, u32[]{:S(2)}, u32[]{:S(2)}) async-start(bf16[1,8,49,768]{3,2,0,1:T(8,128)(2,1)} %fusion.93), calls=%async_computation.3 | async-start | bytes 1376256 | tf_op jit(solution)/shard_map/all_to_all | solution.py:660
  374.9 115.9 %copy-start.48 = (f32[288,128]{1,0:T(8,128)S(1)}, f32[288,128]{1,0:T(8,128)}, u32[]{:S(2)}) copy-start(f32[288,128]{1,0:T(8,128)} %param.25) | copy-start | bytes 442372
  374.9 115.9 %copy-start.55 = (f32[288,128]{1,0:T(8,128)S(1)}, f32[288,128]{1,0:T(8,128)}, u32[]{:S(2)}) copy-start(f32[288,128]{1,0:T(8,128)} %param.26) | copy-start | bytes 442372
  374.9 115.9 %copy-start.56 = (f32[288,128]{1,0:T(8,128)S(1)}, f32[288,128]{1,0:T(8,128)}, u32[]{:S(2)}) copy-start(f32[288,128]{1,0:T(8,128)} %param.27) | copy-start | bytes 442372
  374.9 116.8 %copy-start.54 = (f32[144,128]{1,0:T(8,128)S(1)}, f32[144,128]{1,0:T(8,128)}, u32[]{:S(2)}) copy-start(f32[144,128]{1,0:T(8,128)} %param.28) | copy-start | bytes 221188
  374.9 116.8 %copy-start.59 = (f32[144,128]{1,0:T(8,128)S(1)}, f32[144,128]{1,0:T(8,128)}, u32[]{:S(2)}) copy-start(f32[144,128]{1,0:T(8,128)} %param.29) | copy-start | bytes 221188
  374.9 116.8 %copy-start.60 = (f32[144,128]{1,0:T(8,128)S(1)}, f32[144,128]{1,0:T(8,128)}, u32[]{:S(2)}) copy-start(f32[144,128]{1,0:T(8,128)} %param.30) | copy-start | bytes 221188
  374.9 117.5 %copy-start.67 = (f32[2,3,24]{2,0,1:T(2,128)S(1)}, f32[2,3,24]{2,0,1:T(2,128)}, u32[]{:S(2)}) copy-start(f32[2,3,24]{2,0,1:T(2,128)} %param.37) | copy-start | bytes 1732
  374.9 117.5 %copy-start.68 = (f32[2,3,24]{2,0,1:T(2,128)S(1)}, f32[2,3,24]{2,0,1:T(2,128)}, u32[]{:S(2)}) copy-start(f32[2,3,24]{2,0,1:T(2,128)} %param.38) | copy-start | bytes 1732
  374.9 117.4 %copy-start.69 = (f32[2,3,24]{2,0,1:T(2,128)S(1)}, f32[2,3,24]{2,0,1:T(2,128)}, u32[]{:S(2)}) copy-start(f32[2,3,24]{2,0,1:T(2,128)} %param.39) | copy-start | bytes 1732
  488.2 7.7 %copy-start.35 = (f32[576,128]{1,0:T(8,128)S(1)}, f32[576,128]{1,0:T(8,128)}, u32[]{:S(2)}) copy-start(f32[576,128]{1,0:T(8,128)} %param.31) | copy-start | bytes 884740
  (57 other events, 183.7 us)
